TPU v7x, 32 devices: a whole 2x2x4 slice. The times are simulated.
32 devices in a mesh: groups: 2 (over y), blk: 4 (over z), store: 4 (over x, core).
Axes of the slice: x: 2, y: 2, z: 4, core: 2. Of those that a mesh axis runs over, the one named last changes fastest.
Arguments:
- embeddings: float32 [32768, 1024], P(('groups', 'blk', 'store')), parts along dimension 0, may hold values from -6 to 6
- slots: int32 [32768], P(('groups', 'blk', 'store')), parts along dimension 0, may hold values from 0 to 1023, as said below
- clusters: int32 [8, 4096], P(('groups', 'store'), 'blk'), parts along dimension 0, may hold values from 0 to 31, never falling along the last dimension, each value on 1 to 2048 neighbouring positions
- priority: int32 [8, 4096], P(('groups', 'store'), 'blk'), parts along dimension 0, may hold values from 0 to 4095, each once within a row
Outputs:
- nearest_earlier: float32 [32768], P(('groups', 'blk', 'store')), parts along dimension 0
There are 2 independent parts, one for each index of `groups`. A program takes and returns all parts, laid end to end along the dimension named above; each array names one. Nothing has to cross between parts.
Inputs may be any that keep to these rules, and one draw needn't show every extreme that they name: For each panel of each owner, the slots of the 1024 storage rows bound for it are 0 to 1023, each once. `clusters`: in each owner's row the cluster numbers never fall, every number is used, and a cluster holds 1 to 2048 items, one exactly 2048. `priority`: each owner's row is a permutation.
All inputs are finite; a program needn't handle non-finite values.
Results may differ from a plain program's by a relative error of at most 0.0011.
Values may be sent and summed in bfloat16 or wider, within the bound.
A program may use at most 64 MiB of HBM per device.

v0:
```python
import jax
import jax.numpy as jnp
from jax import lax
from jax.sharding import PartitionSpec as P

SPAN = 2


EPS = 1e-06


def passed_along(shard, axis, by):
    peers = lax.axis_size(axis)
    pairs = [(i, i + by) for i in range(peers) if 0 <= i + by < peers]
    return lax.ppermute(shard, axis, pairs)


def normalize_rows(embeddings):
    return (
        embeddings * lax.rsqrt(jnp.sum(embeddings * embeddings, axis=1, keepdims=True) + EPS)
    ).astype(jnp.bfloat16)


def pair_scores(left_rows, right_rows):
    return lax.dot_general(
        left_rows, right_rows, (((1,), (1,)), ((), ())), preferred_element_type=jnp.float32
    )


def earlier_best(scores, tags_left, order_left, tags_right, order_right):
    same_pair = (tags_left[:, None] == tags_right[None, :]) & (
        order_right[None, :] < order_left[:, None]
    )
    return jnp.max(jnp.where(same_pair, scores, -1.0), axis=1)


def compare(current, visitor):
    scores = pair_scores(current[0], visitor[0])
    row_best = earlier_best(scores, current[1], current[2], visitor[1], visitor[2])
    return (row_best, row_best)


def neighbours(current, direction):
    fetched = []
    for distance in range(1, SPAN + 1):
        fetched.append(
            passed_along((current[0], current[1], current[2]), "blk", direction * distance)
        )
    return fetched


def body(embeddings, slots, clusters, priority):
    unit_rows = normalize_rows(embeddings)
    arrived, places = (
        lax.all_to_all(unit_rows, "store", split_axis=0, concat_axis=0, tiled=True),
        lax.all_to_all(slots, "store", split_axis=0, concat_axis=0, tiled=True),
    )
    placed = jnp.zeros_like(arrived).at[places].set(arrived)
    current = (placed, clusters[0] + 1, priority[0])
    nearest = earlier_best(
        pair_scores(placed, placed), current[1], current[2], current[1], current[2]
    )
    higher = neighbours(current, -1)
    for visitor in higher + neighbours(current, 1):
        row_best, unused = compare(current, visitor)
        nearest = jnp.maximum(nearest, row_best)
    home_best = lax.all_to_all(nearest[places], "store", split_axis=0, concat_axis=0, tiled=True)
    return home_best


def solution(mesh):
    return jax.shard_map(
        body,
        mesh=mesh,
        in_specs=(
            P(("groups", "blk", "store"), None),
            P(("groups", "blk", "store")),
            P(("groups", "store"), "blk"),
            P(("groups", "store"), "blk"),
        ),
        out_specs=P(("groups", "blk", "store")),
        check_vma=False,
    )
```

profile of v0, /device:TPU:0, one launch (start us, length us, event | category | flops | bytes accessed | tf_op | source)
XLA Modules:
  0.0 223.4 jit_solution(723812552072309118)
XLA Ops:
  0.0 4.2 %all-to-all-start = ((s32[4,256,1]{1,2,0:T(1,128)}), s32[4,256,1]{1,2,0:T(1,128)S(1)}, u32[]{:S(2)}, u32[]{:S(2)}) async-start(s32[4,256,1]{1,2,0:T(1,128)} %bitcast.25), calls=%async_computation | async-start | bytes 8192 | tf_op jit(solution)/shard_map/all_to_all | solution.py:56
  4.2 0.0 copy-start
  4.2 2.7 %multiply_reduce_fusion = f32[1024]{0:T(1024)S(1)} fusion(f32[1024,1024]{1,0:T(8,128)} %param.4), kind=kLoop, calls=%fused_computation.8 | loop fusion | flops 2096128 | bytes 4198400 | tf_op jit(solution)/shard_map/reduce_sum | solution.py:20
  6.9 0.8 copy-done
  7.7 1.6 multiply_convert_fusion
  9.3 0.0 all-to-all-done
  9.3 3.6 %all-to-all-start.1 = ((bf16[4,256,1024]{2,1,0:T(8,128)(2,1)}), bf16[4,256,1024]{2,1,0:T(8,128)(2,1)S(1)}, u32[]{:S(2)}, u32[]{:S(2)}) async-start(bf16[4,256,1024]{2,1,0:T(8,128)(2,1)} %bitcast.5), calls=%async_computation.1 | async-start | bytes 4194304 | tf_op jit(solution)/shard_map/all_to_all | solution.py:55
  12.9 0.0 copy-start.2
  12.9 0.0 copy-start.3
  12.9 25.6 %all-to-all-done.1 = bf16[4,256,1024]{2,1,0:T(8,128)(2,1)S(1)} async-done(((bf16[4,256,1024]{2,1,0:T(8,128)(2,1)}), bf16[4,256,1024]{2,1,0:T(8,128)(2,1)S(1)}, u32[]{:S(2)}, u32[]{:S(2)}) %all-to-all-start.1) | async-done | bytes 2097184 | tf_op jit(solution)/shard_map/all_to_all | solution.py:55
  38.6 0.0 copy-start.1
  38.6 1.3 copy-done.1
  39.9 6.6 %scatter_custom_fusion = bf16[1024,1024]{1,0:T(8,128)(2,1)S(1)} fusion(s32[1024]{0:T(1024)S(1)} %bitcast.20, bf16[1024,1024]{1,0:T(8,128)(2,1)} %bitcast.19, bf16[]{:T(256)} %constant.1.clone.1), kind=kCustom, calls=%fused_computation.9 | custom fusion | bytes 2097664 | tf_op jit(solution)/shard_map/scatter | solution.py:58
  46.5 4.1 %collective-permute-start.8 = (bf16[1024,1024]{1,0:T(8,128)(2,1)S(1)}, bf16[1024,1024]{1,0:T(8,128)(2,1)S(1)}, u32[]{:S(2)}, u32[]{:S(2)}) collective-permute-start(bf16[1024,1024]{1,0:T(8,128)(2,1)S(1)} %scatter_custom_fusion), channel_id=1, source_target_pairs={{0,4},{4,8},{8,12},{1,5},{5,9},{9,13},{2,6},{6,10},{10,14},{3,7},{... | collective-permute-start | bytes 6291464 | tf_op jit(solution)/shard_map/ppermute | solution.py:15
  50.6 4.5 %collective-permute-start.11 = (bf16[1024,1024]{1,0:T(8,128)(2,1)S(1)}, bf16[1024,1024]{1,0:T(8,128)(2,1)S(1)}, u32[]{:S(2)}, u32[]{:S(2)}) collective-permute-start(bf16[1024,1024]{1,0:T(8,128)(2,1)S(1)} %scatter_custom_fusion), channel_id=1, source_target_pairs={{0,8},{4,12},{1,9},{5,13},{2,10},{6,14},{3,11},{7,15},{16,24},{20,... | collective-permute-start | bytes 6291464 | tf_op jit(solution)/shard_map/ppermute | solution.py:15
  55.1 1.3 collective-permute-start.5
  56.4 0.0 copy-done.2
  56.4 1.3 collective-permute-start
  57.8 1.3 collective-permute-start.2
  59.1 0.0 copy-done.3
  59.1 2.7 %select_reduce_fusion.4 = f32[1024]{0:T(1024)S(1)} fusion(s32[1024]{0:T(1024)S(1)} %bitcast.32, s32[1024]{0:T(1024)S(1)} %bitcast.27, bf16[1024,1024]{1,0:T(8,128)(2,1)S(1)} %scatter_custom_fusion), kind=kOutput, calls=%fused_computation.6 | convolution fusion | flops 2152725504 | bytes 2109440 | tf_op jit(solution)/shard_map/dot_general | solution.py:25
  61.8 34.7 %collective-permute-done.8 = bf16[1024,1024]{1,0:T(8,128)(2,1)S(1)} collective-permute-done((bf16[1024,1024]{1,0:T(8,128)(2,1)S(1)}, bf16[1024,1024]{1,0:T(8,128)(2,1)S(1)}, u32[]{:S(2)}, u32[]{:S(2)}) %collective-permute-start.8) | collective-permute-done | bytes 2097184 | tf_op jit(solution)/shard_map/ppermute | solution.py:15
  96.5 1.3 collective-permute-start.3
  97.8 2.4 %fusion.3 = f32[1024,1024]{0,1:T(8,128)S(1)} fusion(bf16[1024,1024]{1,0:T(8,128)(2,1)S(1)} %scatter_custom_fusion, bf16[1024,1024]{1,0:T(8,128)(2,1)S(1)} %collective-permute-done.8), kind=kOutput, calls=%fused_computation.17 | convolution fusion | flops 2147483648 | bytes 8388608 | tf_op jit(solution)/shard_map/dot_general | solution.py:25
  100.2 0.0 collective-permute-done
  100.2 51.1 %collective-permute-start.6 = (s32[1024]{0:T(1024)S(1)}, s32[1024]{0:T(1024)S(1)}, u32[]{:S(2)}, u32[]{:S(2)}) collective-permute-start(s32[1024]{0:T(1024)S(1)} %bitcast.29), channel_id=1, source_target_pairs={{0,4},{4,8},{8,12},{1,5},{5,9},{9,13},{2,6},{6,10},{10,14},{3,7},{... | collective-permute-start | bytes 12296 | tf_op jit(solution)/shard_map/ppermute | solution.py:15
  151.3 0.0 collective-permute-done.11
  151.3 2.8 %collective-permute-start.9 = (s32[1024]{0:T(1024)S(1)}, s32[1024]{0:T(1024)S(1)}, u32[]{:S(2)}, u32[]{:S(2)}) collective-permute-start(s32[1024]{0:T(1024)S(1)} %bitcast.30), channel_id=1, source_target_pairs={{0,8},{4,12},{1,9},{5,13},{2,10},{6,14},{3,11},{7,15},{16,24},{20,... | collective-permute-start | bytes 12296 | tf_op jit(solution)/shard_map/ppermute | solution.py:15
  154.1 2.4 %fusion.4 = f32[1024,1024]{0,1:T(8,128)S(1)} fusion(bf16[1024,1024]{1,0:T(8,128)(2,1)S(1)} %scatter_custom_fusion, bf16[1024,1024]{1,0:T(8,128)(2,1)S(1)} %collective-permute-done.11), kind=kOutput, calls=%fused_computation.18 | convolution fusion | flops 2147483648 | bytes 8388608 | tf_op jit(solution)/shard_map/dot_general | solution.py:25
  156.5 37.3 %collective-permute-done.3 = s32[1024]{0:T(1024)S(1)} collective-permute-done((s32[1024]{0:T(1024)S(1)}, s32[1024]{0:T(1024)S(1)}, u32[]{:S(2)}, u32[]{:S(2)}) %collective-permute-start.3) | collective-permute-done | bytes 4128 | tf_op jit(solution)/shard_map/ppermute | solution.py:15
  193.8 1.3 collective-permute-start.1
  195.1 0.0 collective-permute-done.6
  195.1 4.6 %collective-permute-start.10 = (s32[1024]{0:T(1024)S(1)}, s32[1024]{0:T(1024)S(1)}, u32[]{:S(2)}, u32[]{:S(2)}) collective-permute-start(s32[1024]{0:T(1024)S(1)} %bitcast.34), channel_id=1, source_target_pairs={{0,8},{4,12},{1,9},{5,13},{2,10},{6,14},{3,11},{7,15},{16,24},{20,... | collective-permute-start | bytes 12296 | tf_op jit(solution)/shard_map/ppermute | solution.py:15
  199.7 0.0 collective-permute-done.9
  199.8 1.3 collective-permute-start.4
  201.1 0.0 collective-permute-done.5
  201.1 1.6 collective-permute-start.7
  202.7 2.4 %fusion.2 = f32[1024,1024]{0,1:T(8,128)S(1)} fusion(bf16[1024,1024]{1,0:T(8,128)(2,1)S(1)} %scatter_custom_fusion, bf16[1024,1024]{1,0:T(8,128)(2,1)S(1)} %collective-permute-done.5), kind=kOutput, calls=%fused_computation.16 | convolution fusion | flops 2147483648 | bytes 8388608 | tf_op jit(solution)/shard_map/dot_general | solution.py:25
  205.0 0.0 collective-permute-done.1
  205.0 0.0 collective-permute-done.10
  205.1 1.1 collective-permute-done.4
  206.2 0.0 collective-permute-done.7
  206.2 0.0 collective-permute-done.2
  206.2 6.0 %select_reduce_fusion.3 = (f32[1024]{0:T(1024)S(1)}, f32[1024]{0:T(1024)S(1)}, f32[1024]{0:T(1024)S(1)}, f32[1024]{0:T(1024)S(1)}) fusion(s32[1024]{0:T(1024)S(1)} %bitcast.37, s32[1024]{0:T(1024)S(1)} %bitcast.31, s32[1024]{0:T(1024)S(1)} %collective-permute-done.1, s32[1024]{0:T(1024)S(1)} %collective-permute-done, f32[1024,1024]{0,1:T(8,128)S(1)} %fusion.2, ...), kind=kOutput, calls=%fused_computation.5 | convolution fusion | flops 2168451072 | bytes 16834560 | tf_op jit(solution)/shard_map/dot_general | solution.py:25
  212.1 4.5 %gather_fusion = f32[1024]{0:T(1024)S(1)} fusion(f32[1024]{0:T(1024)S(1)} %maximum_maximum_fusion, s32[1024]{0:T(1024)S(1)} %broadcast_clamp_fusion), kind=kCustom, calls=%fused_computation | custom fusion | bytes 12288 | tf_op jit(solution)/shard_map/gather | solution.py:67
  216.7 6.1 %all_to_all.36 = f32[4,256,1]{1,2,0:T(1,128)S(1)} all-to-all(f32[4,256,1]{1,2,0:T(1,128)S(1)} %bitcast.24), channel_id=1, replica_groups=mesh['groups'=2,'blk'=4,'store'=4] {'store'}, dimensions={0} | all-to-all | bytes 8192 | tf_op jit(solution)/shard_map/all_to_all | solution.py:67
  222.8 0.6 copy.8
  (5 shorter events, 0.0 us)
Async XLA Ops:
  0.0 9.3 %all-to-all-start = ((s32[4,256,1]{1,2,0:T(1,128)}), s32[4,256,1]{1,2,0:T(1,128)S(1)}, u32[]{:S(2)}, u32[]{:S(2)}) async-start(s32[4,256,1]{1,2,0:T(1,128)} %bitcast.25), calls=%async_computation | async-start | bytes 8192 | tf_op jit(solution)/shard_map/all_to_all | solution.py:56
  4.2 3.4 %copy-start = (f32[1024,1024]{1,0:T(8,128)S(1)}, f32[1024,1024]{1,0:T(8,128)}, u32[]{:S(2)}) copy-start(f32[1024,1024]{1,0:T(8,128)} %param.4) | copy-start | bytes 12582916
  9.3 29.3 %all-to-all-start.1 = ((bf16[4,256,1024]{2,1,0:T(8,128)(2,1)}), bf16[4,256,1024]{2,1,0:T(8,128)(2,1)S(1)}, u32[]{:S(2)}, u32[]{:S(2)}) async-start(bf16[4,256,1024]{2,1,0:T(8,128)(2,1)} %bitcast.5), calls=%async_computation.1 | async-start | bytes 4194304 | tf_op jit(solution)/shard_map/all_to_all | solution.py:55
  12.9 43.5 %copy-start.2 = (s32[1,1024]{1,0:T(1,128)S(1)}, s32[1,1024]{1,0:T(1,128)}, u32[]{:S(2)}) copy-start(s32[1,1024]{1,0:T(1,128)} %param.6) | copy-start | bytes 12292
  12.9 46.1 %copy-start.3 = (s32[1,1024]{1,0:T(1,128)S(1)}, s32[1,1024]{1,0:T(1,128)}, u32[]{:S(2)}) copy-start(s32[1,1024]{1,0:T(1,128)} %param.7) | copy-start | bytes 12292
  38.6 1.3 copy-start.1
  46.5 50.0 %collective-permute-start.8 = (bf16[1024,1024]{1,0:T(8,128)(2,1)S(1)}, bf16[1024,1024]{1,0:T(8,128)(2,1)S(1)}, u32[]{:S(2)}, u32[]{:S(2)}) collective-permute-start(bf16[1024,1024]{1,0:T(8,128)(2,1)S(1)} %scatter_custom_fusion), channel_id=1, source_target_pairs={{0,4},{4,8},{8,12},{1,5},{5,9},{9,13},{2,6},{6,10},{10,14},{3,7},{... | collective-permute-start | bytes 6291464 | tf_op jit(solution)/shard_map/ppermute | solution.py:15
  50.6 100.7 %collective-permute-start.11 = (bf16[1024,1024]{1,0:T(8,128)(2,1)S(1)}, bf16[1024,1024]{1,0:T(8,128)(2,1)S(1)}, u32[]{:S(2)}, u32[]{:S(2)}) collective-permute-start(bf16[1024,1024]{1,0:T(8,128)(2,1)S(1)} %scatter_custom_fusion), channel_id=1, source_target_pairs={{0,8},{4,12},{1,9},{5,13},{2,10},{6,14},{3,11},{7,15},{16,24},{20,... | collective-permute-start | bytes 6291464 | tf_op jit(solution)/shard_map/ppermute | solution.py:15
  55.1 145.9 %collective-permute-start.5 = (bf16[1024,1024]{1,0:T(8,128)(2,1)S(1)}, bf16[1024,1024]{1,0:T(8,128)(2,1)S(1)}, u32[]{:S(2)}, u32[]{:S(2)}) collective-permute-start(bf16[1024,1024]{1,0:T(8,128)(2,1)S(1)} %scatter_custom_fusion), channel_id=1, source_target_pairs={{8,0},{12,4},{9,1},{13,5},{10,2},{14,6},{11,3},{15,7},{24,16},{28,... | collective-permute-start | bytes 6291464 | tf_op jit(solution)/shard_map/ppermute | solution.py:15
  56.4 43.8 %collective-permute-start = (s32[1024]{0:T(1024)S(1)}, s32[1024]{0:T(1024)S(1)}, u32[]{:S(2)}, u32[]{:S(2)}) collective-permute-start(s32[1024]{0:T(1024)S(1)} %bitcast.26), channel_id=1, source_target_pairs={{4,0},{8,4},{12,8},{5,1},{9,5},{13,9},{6,2},{10,6},{14,10},{7,3},{... | collective-permute-start | bytes 12296 | tf_op jit(solution)/shard_map/ppermute | solution.py:15
  57.8 148.4 %collective-permute-start.2 = (bf16[1024,1024]{1,0:T(8,128)(2,1)S(1)}, bf16[1024,1024]{1,0:T(8,128)(2,1)S(1)}, u32[]{:S(2)}, u32[]{:S(2)}) collective-permute-start(bf16[1024,1024]{1,0:T(8,128)(2,1)S(1)} %scatter_custom_fusion), channel_id=1, source_target_pairs={{4,0},{8,4},{12,8},{5,1},{9,5},{13,9},{6,2},{10,6},{14,10},{7,3},{... | collective-permute-start | bytes 6291464 | tf_op jit(solution)/shard_map/ppermute | solution.py:15
  96.5 97.3 %collective-permute-start.3 = (s32[1024]{0:T(1024)S(1)}, s32[1024]{0:T(1024)S(1)}, u32[]{:S(2)}, u32[]{:S(2)}) collective-permute-start(s32[1024]{0:T(1024)S(1)} %bitcast.28), channel_id=1, source_target_pairs={{8,0},{12,4},{9,1},{13,5},{10,2},{14,6},{11,3},{15,7},{24,16},{28,... | collective-permute-start | bytes 12296 | tf_op jit(solution)/shard_map/ppermute | solution.py:15
  100.2 94.9 %collective-permute-start.6 = (s32[1024]{0:T(1024)S(1)}, s32[1024]{0:T(1024)S(1)}, u32[]{:S(2)}, u32[]{:S(2)}) collective-permute-start(s32[1024]{0:T(1024)S(1)} %bitcast.29), channel_id=1, source_target_pairs={{0,4},{4,8},{8,12},{1,5},{5,9},{9,13},{2,6},{6,10},{10,14},{3,7},{... | collective-permute-start | bytes 12296 | tf_op jit(solution)/shard_map/ppermute | solution.py:15
  151.3 48.4 %collective-permute-start.9 = (s32[1024]{0:T(1024)S(1)}, s32[1024]{0:T(1024)S(1)}, u32[]{:S(2)}, u32[]{:S(2)}) collective-permute-start(s32[1024]{0:T(1024)S(1)} %bitcast.30), channel_id=1, source_target_pairs={{0,8},{4,12},{1,9},{5,13},{2,10},{6,14},{3,11},{7,15},{16,24},{20,... | collective-permute-start | bytes 12296 | tf_op jit(solution)/shard_map/ppermute | solution.py:15
  193.8 11.2 %collective-permute-start.1 = (s32[1024]{0:T(1024)S(1)}, s32[1024]{0:T(1024)S(1)}, u32[]{:S(2)}, u32[]{:S(2)}) collective-permute-start(s32[1024]{0:T(1024)S(1)} %bitcast.33), channel_id=1, source_target_pairs={{4,0},{8,4},{12,8},{5,1},{9,5},{13,9},{6,2},{10,6},{14,10},{7,3},{... | collective-permute-start | bytes 12296 | tf_op jit(solution)/shard_map/ppermute | solution.py:15
  195.1 9.9 %collective-permute-start.10 = (s32[1024]{0:T(1024)S(1)}, s32[1024]{0:T(1024)S(1)}, u32[]{:S(2)}, u32[]{:S(2)}) collective-permute-start(s32[1024]{0:T(1024)S(1)} %bitcast.34), channel_id=1, source_target_pairs={{0,8},{4,12},{1,9},{5,13},{2,10},{6,14},{3,11},{7,15},{16,24},{20,... | collective-permute-start | bytes 12296 | tf_op jit(solution)/shard_map/ppermute | solution.py:15
  199.8 6.4 %collective-permute-start.4 = (s32[1024]{0:T(1024)S(1)}, s32[1024]{0:T(1024)S(1)}, u32[]{:S(2)}, u32[]{:S(2)}) collective-permute-start(s32[1024]{0:T(1024)S(1)} %bitcast.35), channel_id=1, source_target_pairs={{8,0},{12,4},{9,1},{13,5},{10,2},{14,6},{11,3},{15,7},{24,16},{28,... | collective-permute-start | bytes 12296 | tf_op jit(solution)/shard_map/ppermute | solution.py:15
  201.1 5.1 %collective-permute-start.7 = (s32[1024]{0:T(1024)S(1)}, s32[1024]{0:T(1024)S(1)}, u32[]{:S(2)}, u32[]{:S(2)}) collective-permute-start(s32[1024]{0:T(1024)S(1)} %bitcast.36), channel_id=1, source_target_pairs={{0,4},{4,8},{8,12},{1,5},{5,9},{9,13},{2,6},{6,10},{10,14},{3,7},{... | collective-permute-start | bytes 12296 | tf_op jit(solution)/shard_map/ppermute | solution.py:15
where the time goes:
time: 224 us; the launch traced here: 223 us
  waiting for transfers between devices  98.8 us (44%)
  starting transfers between devices  84.2 us (38%)
  matrix products  15.8 us (7%)
  local copies, waits for them, and re-layouts  13.8 us (6%)
  blocking collectives  6.13 us (3%)
  other arithmetic  4.34 us (2%)
    ppermute x12, starting transfers between devices, passed_along(): return lax.ppermute(shard, axis, pairs)  76.4 us
    ppermute x12, waiting for transfers between devices, passed_along(): return lax.ppermute(shard, axis, pairs)  73.2 us
    all_to_all x1, waiting for transfers between devices, body(): lax.all_to_all(unit_rows, 'store', split_axis=0, concat_axis=0, tiled=True)  25.6 us
    dot_general x5, matrix products, pair_scores(): lax.dot_general(left_rows, right_rows, (((1,), (1,)), ((), ())), preferre...  15.8 us
    scatter x1, local copies, waits for them, and re-layouts, body(): placed = jnp.zeros_like(arrived).at[places].set(arrived)  6.58 us
    all_to_all x1, blocking collectives, body(): lax.all_to_all(nearest[places], 'store', split_axis=0, concat_axis=0, til...  6.13 us
    gather x1, local copies, waits for them, and re-layouts, body(): nearest[places]  4.53 us
  transfers between devices with their start and end apart: 14, of which 4 were waited for; matrix products, arithmetic and copies ran while one was open for 6% of the time, Pallas kernels for 0%

commit v1 on v0

v1 whole, which is shorter than its diff:
```python
import functools

import jax
import jax.numpy as jnp
from jax import lax
from jax.experimental import pallas as pl
from jax.experimental.pallas import tpu as pltpu
from jax.sharding import PartitionSpec as P

EPS = 1e-06
MESH = pl.DeviceIdType.MESH


def kernel(
    panels,
    stores,
    emb_ref,
    slots_ref,
    cl_ref,
    pr_ref,
    out_ref,
    emb,
    mine,
    left,
    right,
    bound,
    slots_in,
    tag_mine,
    tag_left,
    tag_right,
    clcol_mine,
    prcol_mine,
    clcol_left,
    prcol_left,
    row_mine,
    row_left,
    col_mine,
    col_right,
    back_mine,
    back_left,
    back_right,
    home,
    load_sem,
    st_send,
    st_recv,
    sl_send,
    sl_recv,
    tg_send,
    tg_recv,
    zl_send,
    zl_recv,
    zr_send,
    zr_recv,
    bk_send,
    bk_recv,
):
    rows, width = emb.shape[0] * emb.shape[1], emb.shape[2]
    send = rows // stores
    half = stores // 2
    p = lax.axis_index("blk")
    s = lax.axis_index("store")

    def out_peer(d):
        return lax.rem(s // 2 + d // 2, half) * 2 + lax.rem(lax.rem(s, 2) + d % 2, 2)

    def in_peer(d):
        return lax.rem(s // 2 + half - d // 2, half) * 2 + lax.rem(lax.rem(s, 2) + d % 2, 2)

    has_prev = p >= 1
    has_next = p <= panels - 2
    use_right = has_next
    use_left = jnp.logical_and(has_prev, has_next)
    give_right = p <= panels - 3
    give_left = has_prev

    barrier = pltpu.get_barrier_semaphore()
    for d in range(1, stores):
        pl.semaphore_signal(barrier, inc=1, device_id={"store": out_peer(d)}, device_id_type=MESH)

    @pl.when(has_prev)
    def _():
        for d in range(stores):
            pl.semaphore_signal(
                barrier, inc=1, device_id={"blk": p - 1, "store": out_peer(d)}, device_id_type=MESH
            )

    @pl.when(has_next)
    def _():
        for d in range(stores):
            pl.semaphore_signal(
                barrier, inc=1, device_id={"blk": p + 1, "store": out_peer(d)}, device_id_type=MESH
            )

    order = [2, 0, 1] + list(range(3, stores)) if stores > 2 else [0, 1]

    def load(d):
        return pltpu.make_async_copy(
            emb_ref.at[pl.ds(pl.multiple_of(out_peer(d) * send, send), send)],
            emb.at[d],
            load_sem.at[d],
        )

    for d in order:
        load(d).start()

    low = jnp.full((1, send), -1.0, jnp.float32)
    for k in range(3):
        for o in range(stores):
            home[k, o] = low
    for ref in (row_mine, row_left):
        ref[...] = jnp.full(ref.shape, -1.0, jnp.float32)
    for ref in (col_mine, col_right):
        ref[...] = jnp.full(ref.shape, -1.0, jnp.float32)

    def store_copy(d):
        return pltpu.make_async_remote_copy(
            src_ref=bound.at[d],
            dst_ref=mine.at[d],
            send_sem=st_send.at[d],
            recv_sem=st_recv.at[d],
            device_id={"store": out_peer(d)},
            device_id_type=MESH,
        )

    def slot_copy(d):
        return pltpu.make_async_remote_copy(
            src_ref=slots_ref.at[:, pl.ds(pl.multiple_of(out_peer(d) * send, send), send)],
            dst_ref=slots_in.at[d],
            send_sem=sl_send.at[d],
            recv_sem=sl_recv.at[d],
            device_id={"store": out_peer(d)},
            device_id_type=MESH,
        )

    def to_left(d):
        return pltpu.make_async_remote_copy(
            src_ref=mine.at[d],
            dst_ref=right.at[d],
            send_sem=zl_send.at[d],
            recv_sem=zl_recv.at[d],
            device_id={"blk": p - 1},
            device_id_type=MESH,
        )

    def to_right(d):
        return pltpu.make_async_remote_copy(
            src_ref=mine.at[d],
            dst_ref=left.at[d],
            send_sem=zr_send.at[d],
            recv_sem=zr_recv.at[d],
            device_id={"blk": p + 1},
            device_id_type=MESH,
        )

    def tag_copy(to_next):
        return pltpu.make_async_remote_copy(
            src_ref=tag_mine,
            dst_ref=tag_left if to_next else tag_right,
            send_sem=tg_send.at[1 if to_next else 0],
            recv_sem=tg_recv.at[1 if to_next else 0],
            device_id={"blk": p + 1 if to_next else p - 1},
            device_id_type=MESH,
        )

    def forward(d):
        @pl.when(give_right)
        def _():
            to_right(d).start()

        @pl.when(give_left)
        def _():
            to_left(d).start()

    def normalize(d):
        load(d).wait()
        x = emb[d]
        unit = (x * lax.rsqrt(jnp.sum(x * x, axis=1, keepdims=True) + EPS)).astype(jnp.bfloat16)
        if d == 0:
            mine[0] = unit
        else:
            bound[d] = unit

    for number, d in enumerate(order):
        normalize(d)
        if number == 0:
            here = jnp.int32(stores - 1)
            here = here + jnp.where(has_prev, stores, 0) + jnp.where(has_next, stores, 0)
            pl.semaphore_wait(barrier, here)
            for e in range(1, stores):
                slot_copy(e).start()
        if d == 0:
            forward(0)
        else:
            store_copy(d).start()

    clusters = cl_ref[...].astype(jnp.float32)
    rank = pr_ref[...]
    upper = (rank // 128).astype(jnp.float32)
    lower = (rank - rank // 128 * 128).astype(jnp.float32)
    line = lax.broadcasted_iota(jnp.int32, (16, rows), 0)
    table = jnp.where(
        line == 0, clusters, jnp.where(line == 1, upper, jnp.where(line == 2, lower, 0.0))
    ).astype(jnp.bfloat16)

    def columns(tag_ref, clcol, prcol, d):
        clcol[d] = jnp.transpose(jnp.broadcast_to(tag_ref[d, 0:1, :], (128, send)))
        prcol[d] = jnp.transpose(jnp.broadcast_to(tag_ref[d, 1:2, :], (128, send)))

    slots_in[0] = slots_ref[:, pl.ds(pl.multiple_of(s * send, send), send)]
    for d in range(stores):
        if d > 0:
            slot_copy(d).wait()
        hot = jnp.where(
            lax.broadcasted_iota(jnp.int32, (rows, send), 0) == slots_in[d], 1.0, 0.0
        ).astype(jnp.bfloat16)
        found = jnp.dot(table, hot, preferred_element_type=jnp.float32)
        tag_mine[d] = jnp.concatenate(
            [found[0:1], found[1:2] * 128.0 + found[2:3], found[2:8]], axis=0
        )
        columns(tag_mine, clcol_mine, prcol_mine, d)

    @pl.when(give_right)
    def _():
        tag_copy(True).start()

    @pl.when(give_left)
    def _():
        tag_copy(False).start()

    def pair(a_ref, i, clcol, prcol, row_acc, b_ref, j, tag_ref, col_acc):
        scores = lax.dot_general(
            a_ref[i], b_ref[j], (((1,), (1,)), ((), ())), preferred_element_type=jnp.float32
        )
        cl_r, pr_r = clcol[i], prcol[i]
        best = row_acc[i]
        for k in range(send // 128):
            part = slice(k * 128, (k + 1) * 128)
            cl_q = tag_ref[j, 0:1, part]
            pr_q = tag_ref[j, 1:2, part]
            same = jnp.where(cl_r == cl_q, scores[:, part], -1.0)
            best = jnp.maximum(best, jnp.where(pr_q < pr_r, same, -1.0))
            other = jnp.where(pr_q > pr_r, same, -1.0)
            top = jnp.max(other.reshape(send // 8, 8, 128), axis=0)
            col_acc[j, :, part] = jnp.maximum(col_acc[j, :, part], top)
        row_acc[i] = best

    def loop(count, step):
        def each(i, carry):
            step(i)
            return carry

        lax.fori_loop(0, count, each, 0)

    for d in range(stores):
        if d > 0:
            store_copy(d).wait_recv()
            forward(d)
        loop(
            d + 1,
            lambda i, d=d: pair(
                mine, i, clcol_mine, prcol_mine, row_mine, mine, d, tag_mine, col_mine
            ),
        )

    def finish(acc_row, acc_col, d):
        parts = []
        if acc_row is not None:
            parts.append(jnp.max(jnp.transpose(acc_row[d]), axis=0, keepdims=True))
        if acc_col is not None:
            parts.append(jnp.max(acc_col[d], axis=0, keepdims=True))
        return functools.reduce(jnp.maximum, parts)

    def back_copy(kind, src, d):
        where = {"store": in_peer(d)}
        if kind:
            where["blk"] = p + 1 if kind == 1 else p - 1
        return pltpu.make_async_remote_copy(
            src_ref=src.at[d],
            dst_ref=home.at[kind, s],
            send_sem=bk_send.at[kind, d],
            recv_sem=bk_recv.at[kind, s],
            device_id=where,
            device_id_type=MESH,
        )

    @pl.when(use_left)
    def _():
        tag_copy(True).wait_recv()
        for d in range(stores):
            columns(tag_left, clcol_left, prcol_left, d)

    @pl.when(use_right)
    def _():
        tag_copy(False).wait_recv()

    for d in range(stores):

        @pl.when(use_right)
        def _(d=d):
            to_left(d).wait_recv()
            loop(
                stores,
                lambda i: pair(
                    mine, i, clcol_mine, prcol_mine, row_mine, right, d, tag_right, col_right
                ),
            )

        if d == stores - 1:
            for e in range(stores):
                back_mine[e] = finish(row_mine, col_mine, e)
            for e in range(1, stores):
                back_copy(0, back_mine, e).start()
            home[0, s] = back_mine[0]

        @pl.when(use_left)
        def _(d=d):
            to_right(d).wait_recv()
            loop(
                d + 1,
                lambda i: pair(
                    left, i, clcol_left, prcol_left, row_left, right, d, tag_right, col_right
                ),
            )
            if d > 0:
                loop(
                    d,
                    lambda j: pair(
                        left, d, clcol_left, prcol_left, row_left, right, j, tag_right, col_right
                    ),
                )

    @pl.when(use_right)
    def _():
        for e in range(stores):
            back_right[e] = finish(None, col_right, e)
            back_copy(1, back_right, e).start()

    @pl.when(use_left)
    def _():
        for e in range(stores):
            back_left[e] = finish(row_left, None, e)
            back_copy(2, back_left, e).start()

    for d in range(1, stores):
        store_copy(d).wait_send()

    @pl.when(give_right)
    def _():
        tag_copy(True).wait_send()
        for d in range(stores):
            to_right(d).wait_send()

    @pl.when(give_left)
    def _():
        tag_copy(False).wait_send()
        for d in range(stores):
            to_left(d).wait_send()

    def arrived(kind, o):
        return pltpu.make_async_remote_copy(
            src_ref=back_mine.at[0],
            dst_ref=home.at[kind, o],
            send_sem=bk_send.at[kind, 0],
            recv_sem=bk_recv.at[kind, o],
            device_id={"store": out_peer(1)},
            device_id_type=MESH,
        )

    for d in range(1, stores):
        back_copy(0, back_mine, d).wait_send()
        arrived(0, out_peer(d)).wait_recv()

    @pl.when(use_right)
    def _():
        for d in range(stores):
            back_copy(1, back_right, d).wait_send()

    @pl.when(use_left)
    def _():
        for d in range(stores):
            back_copy(2, back_left, d).wait_send()

    @pl.when(has_prev)
    def _():
        for o in range(stores):
            arrived(1, o).wait_recv()

    @pl.when(give_right)
    def _():
        for o in range(stores):
            arrived(2, o).wait_recv()

    for o in range(stores):
        out_ref[:, o * send : (o + 1) * send] = jnp.maximum(
            home[0, o], jnp.maximum(home[1, o], home[2, o])
        )


def solution(mesh):
    panels, stores = mesh.shape["blk"], mesh.shape["store"]

    def body(embeddings, slots, clusters, priority):
        rows, width = embeddings.shape
        send = rows // stores
        f32, bf16, i32 = jnp.float32, jnp.bfloat16, jnp.int32
        vm = pltpu.VMEM
        dma = pltpu.SemaphoreType.DMA
        best = pl.pallas_call(
            functools.partial(kernel, panels, stores),
            out_shape=jax.ShapeDtypeStruct((1, rows), f32),
            in_specs=[
                pl.BlockSpec(memory_space=pl.ANY),
                pl.BlockSpec(memory_space=vm),
                pl.BlockSpec(memory_space=vm),
                pl.BlockSpec(memory_space=vm),
            ],
            out_specs=pl.BlockSpec(memory_space=vm),
            scratch_shapes=[
                vm((stores, send, width), f32),
                vm((stores, send, width), bf16),
                vm((stores, send, width), bf16),
                vm((stores, send, width), bf16),
                vm((stores, send, width), bf16),
                vm((stores, 1, send), i32),
                vm((stores, 8, send), f32),
                vm((stores, 8, send), f32),
                vm((stores, 8, send), f32),
                vm((stores, send, 128), f32),
                vm((stores, send, 128), f32),
                vm((stores, send, 128), f32),
                vm((stores, send, 128), f32),
                vm((stores, send, 128), f32),
                vm((stores, send, 128), f32),
                vm((stores, 8, send), f32),
                vm((stores, 8, send), f32),
                vm((stores, 1, send), f32),
                vm((stores, 1, send), f32),
                vm((stores, 1, send), f32),
                vm((3, stores, 1, send), f32),
                dma((stores,)),
                dma((stores,)),
                dma((stores,)),
                dma((stores,)),
                dma((stores,)),
                dma((2,)),
                dma((2,)),
                dma((stores,)),
                dma((stores,)),
                dma((stores,)),
                dma((stores,)),
                dma((3, stores)),
                dma((3, stores)),
            ],
            compiler_params=pltpu.CompilerParams(
                collective_id=0, has_side_effects=True, vmem_limit_bytes=48 * 1024 * 1024
            ),
            name="dedup",
        )(embeddings, slots.reshape(1, rows), clusters, priority)
        return best.reshape(rows)

    return jax.shard_map(
        body,
        mesh=mesh,
        in_specs=(
            P(("groups", "blk", "store"), None),
            P(("groups", "blk", "store")),
            P(("groups", "store"), "blk"),
            P(("groups", "store"), "blk"),
        ),
        out_specs=P(("groups", "blk", "store")),
        check_vma=False,
    )
```

time: 224 us -> 65.7 us (0.29)
  waiting for transfers between devices: 98.8 us -> 0 us
  starting transfers between devices: 84.2 us -> 0 us
  Pallas kernels: 0 us -> 60.6 us
  matrix products: 15.8 us -> 0 us
  local copies, waits for them, and re-layouts: 13.8 us -> 4.84 us
  blocking collectives: 6.13 us -> 0 us
  other arithmetic: 4.34 us -> 0 us
    ppermute x12 -> x0, starting transfers between devices: 76.4 us -> none  [passed_along(): return lax.ppermute(shard, axis, pairs)]
    ppermute x12 -> x0, waiting for transfers between devices: 73.2 us -> none  [passed_along(): return lax.ppermute(shard, axis, pairs)]
    pallas_call x0 -> x1, Pallas kernels: none -> 60.6 us  [body(): pl.pallas_call(functools.partial(kernel, panels, stores), out_shape=jax.S...]
    all_to_all x2 -> x0, waiting for transfers between devices: 25.6 us -> none  [the longest x1 25.6 us: body(): lax.all_to_all(unit_rows, 'store', split_axis=0, concat_axis=0, tiled=True)]
    dot_general x5 -> x0, matrix products: 15.8 us -> none  [pair_scores(): lax.dot_general(left_rows, right_rows, (((1,), (1,)), ((), ())), preferre...]
    all_to_all x2 -> x0, starting transfers between devices: 7.81 us -> none  [the longest x1 4.21 us: body(): lax.all_to_all(slots, 'store', split_axis=0, concat_axis=0, tiled=True)]
    scatter x1 -> x0, local copies, waits for them, and re-layouts: 6.58 us -> none  [body(): placed = jnp.zeros_like(arrived).at[places].set(arrived)]
    all_to_all x1 -> x0, blocking collectives: 6.13 us -> none  [body(): lax.all_to_all(nearest[places], 'store', split_axis=0, concat_axis=0, til...]
  transfers between devices with their start and end apart: 14 -> 0, of which waited for: 4 -> 0; matrix products, arithmetic and copies ran while one was open for 6% -> 0% of each run, Pallas kernels for 0% -> 0%
where the time goes in v1:
time: 65.7 us; the launch traced here: 65.5 us
  Pallas kernels  60.6 us (92%)
  local copies, waits for them, and re-layouts  4.84 us (7%)
    pallas_call x1, Pallas kernels, body(): pl.pallas_call(functools.partial(kernel, panels, stores), out_shape=jax.S...  60.6 us
    unnamed x9, local copies, waits for them, and re-layouts  4.84 us

profile of v1, /device:TPU:0, one launch (start us, length us, event | category | flops | bytes accessed | tf_op | source)
XLA Modules:
  0.0 65.5 jit_solution(7872464714130614317)
XLA Ops:
  0.0 0.0 copy-start
  0.0 2.2 %copy-done = f32[1024,1024]{1,0:T(8,128)S(1)} copy-done((f32[1024,1024]{1,0:T(8,128)S(1)}, f32[1024,1024]{1,0:T(8,128)}, u32[]{:S(2)}) %copy-start) | copy-done | bytes 4194328
  2.2 0.0 copy-start.1
  2.2 0.7 %copy-done.1 = s32[1024]{0:T(1024)S(1)} copy-done((s32[1024]{0:T(1024)S(1)}, s32[1024]{0:T(1024)}, u32[]{:S(2)}) %copy-start.1) | copy-done | bytes 4120
  2.9 0.0 copy-start.2
  2.9 0.7 %copy-done.2 = s32[1,1024]{1,0:T(1,128)S(1)} copy-done((s32[1,1024]{1,0:T(1,128)S(1)}, s32[1,1024]{1,0:T(1,128)}, u32[]{:S(2)}) %copy-start.2) | copy-done | bytes 4120
  3.6 0.0 copy-start.3
  3.6 0.7 %copy-done.3 = s32[1,1024]{1,0:T(1,128)S(1)} copy-done((s32[1,1024]{1,0:T(1,128)S(1)}, s32[1,1024]{1,0:T(1,128)}, u32[]{:S(2)}) %copy-start.3) | copy-done | bytes 4120
  4.3 60.6 %dedup.1 = f32[1,1024]{1,0:T(1,128)S(1)} custom-call(f32[1024,1024]{1,0:T(8,128)S(1)} %copy-done, s32[1,1024]{1,0:T(1,128)S(1)} %bitcast.3, s32[1,1024]{1,0:T(1,128)S(1)} %copy-done.2, s32[1,1024]{1,0:T(1,128)S(1)} %copy-done.3), custom_call_target="tpu_custom_call" | custom-call | tf_op jit(solution)/shard_map/dedup/pallas_call | solution.py:408
  64.9 0.6 copy.6
Async XLA Ops:
  0.0 2.2 %copy-start = (f32[1024,1024]{1,0:T(8,128)S(1)}, f32[1024,1024]{1,0:T(8,128)}, u32[]{:S(2)}) copy-start(f32[1024,1024]{1,0:T(8,128)} %emb_ref.1) | copy-start | bytes 12582916
  2.2 0.7 %copy-start.1 = (s32[1024]{0:T(1024)S(1)}, s32[1024]{0:T(1024)}, u32[]{:S(2)}) copy-start(s32[1024]{0:T(1024)} %param.5) | copy-start | bytes 12292
  2.9 0.7 %copy-start.2 = (s32[1,1024]{1,0:T(1,128)S(1)}, s32[1,1024]{1,0:T(1,128)}, u32[]{:S(2)}) copy-start(s32[1,1024]{1,0:T(1,128)} %cl_ref.1) | copy-start | bytes 12292
  3.6 0.7 %copy-start.3 = (s32[1,1024]{1,0:T(1,128)S(1)}, s32[1,1024]{1,0:T(1,128)}, u32[]{:S(2)}) copy-start(s32[1,1024]{1,0:T(1,128)} %pr_ref.1) | copy-start | bytes 12292

commit v2 on v1

--- a/solution.py
+++ b/solution.py
@@ -15,10 +15,13 @@
     panels,
     stores,
     emb_ref,
+    slots_hbm,
+    cl_hbm,
+    pr_hbm,
+    out_ref,
     slots_ref,
     cl_ref,
     pr_ref,
-    out_ref,
     emb,
     mine,
     left,
@@ -41,6 +44,7 @@
     back_right,
     home,
     load_sem,
+    small_sem,
     st_send,
     st_recv,
     sl_send,
@@ -91,7 +95,7 @@
                 barrier, inc=1, device_id={"blk": p + 1, "store": out_peer(d)}, device_id_type=MESH
             )
 
-    order = [2, 0, 1] + list(range(3, stores)) if stores > 2 else [0, 1]
+    order = [0, 2, 1] + list(range(3, stores)) if stores > 2 else [0, 1]
 
     def load(d):
         return pltpu.make_async_copy(
@@ -100,8 +104,16 @@
             load_sem.at[d],
         )
 
+    small = [
+        pltpu.make_async_copy(a, b, small_sem.at[k])
+        for k, (a, b) in enumerate(
+            [(slots_hbm, slots_ref), (cl_hbm, cl_ref), (pr_hbm, pr_ref)]
+        )
+    ]
     for d in order:
         load(d).start()
+    for copy in small:
+        copy.start()
 
     low = jnp.full((1, send), -1.0, jnp.float32)
     for k in range(3):
@@ -186,6 +198,7 @@
             here = jnp.int32(stores - 1)
             here = here + jnp.where(has_prev, stores, 0) + jnp.where(has_next, stores, 0)
             pl.semaphore_wait(barrier, here)
+            small[0].wait()
             for e in range(1, stores):
                 slot_copy(e).start()
         if d == 0:
@@ -193,6 +206,8 @@
         else:
             store_copy(d).start()
 
+    small[1].wait()
+    small[2].wait()
     clusters = cl_ref[...].astype(jnp.float32)
     rank = pr_ref[...]
     upper = (rank // 128).astype(jnp.float32)
@@ -227,22 +242,32 @@
     def _():
         tag_copy(False).start()
 
+    def pairs(a_ref, i, n, clcol, prcol, row_acc, b_ref, j, m, tag_ref, col_acc):
+        a = a_ref[pl.ds(i, n)].reshape(n * send, width)
+        b = b_ref[pl.ds(j, m)].reshape(m * send, width)
+        scores = lax.dot_general(
+            a, b, (((1,), (1,)), ((), ())), preferred_element_type=jnp.float32
+        )
+        for x in range(n):
+            cl_r, pr_r = clcol[i + x], prcol[i + x]
+            best = row_acc[i + x]
+            for y in range(m):
+                for k in range(send // 128):
+                    part = slice(k * 128, (k + 1) * 128)
+                    cl_q = tag_ref[j + y, 0:1, part]
+                    pr_q = tag_ref[j + y, 1:2, part]
+                    piece = scores[
+                        x * send : (x + 1) * send, y * send + k * 128 : y * send + (k + 1) * 128
+                    ]
+                    same = jnp.where(cl_r == cl_q, piece, -1.0)
+                    best = jnp.maximum(best, jnp.where(pr_q < pr_r, same, -1.0))
+                    other = jnp.where(pr_q > pr_r, same, -1.0)
+                    top = jnp.max(other.reshape(send // 8, 8, 128), axis=0)
+                    col_acc[j + y, :, part] = jnp.maximum(col_acc[j + y, :, part], top)
+            row_acc[i + x] = best
+
     def pair(a_ref, i, clcol, prcol, row_acc, b_ref, j, tag_ref, col_acc):
-        scores = lax.dot_general(
-            a_ref[i], b_ref[j], (((1,), (1,)), ((), ())), preferred_element_type=jnp.float32
-        )
-        cl_r, pr_r = clcol[i], prcol[i]
-        best = row_acc[i]
-        for k in range(send // 128):
-            part = slice(k * 128, (k + 1) * 128)
-            cl_q = tag_ref[j, 0:1, part]
-            pr_q = tag_ref[j, 1:2, part]
-            same = jnp.where(cl_r == cl_q, scores[:, part], -1.0)
-            best = jnp.maximum(best, jnp.where(pr_q < pr_r, same, -1.0))
-            other = jnp.where(pr_q > pr_r, same, -1.0)
-            top = jnp.max(other.reshape(send // 8, 8, 128), axis=0)
-            col_acc[j, :, part] = jnp.maximum(col_acc[j, :, part], top)
-        row_acc[i] = best
+        pairs(a_ref, i, 1, clcol, prcol, row_acc, b_ref, j, 1, tag_ref, col_acc)
 
     def loop(count, step):
         def each(i, carry):
@@ -293,7 +318,8 @@
     def _():
         tag_copy(False).wait_recv()
 
-    for d in range(stores):
+    last = stores - 1
+    for d in range(last):
 
         @pl.when(use_right)
         def _(d=d):
@@ -304,13 +330,6 @@
                     mine, i, clcol_mine, prcol_mine, row_mine, right, d, tag_right, col_right
                 ),
             )
-
-        if d == stores - 1:
-            for e in range(stores):
-                back_mine[e] = finish(row_mine, col_mine, e)
-            for e in range(1, stores):
-                back_copy(0, back_mine, e).start()
-            home[0, s] = back_mine[0]
 
         @pl.when(use_left)
         def _(d=d):
@@ -331,6 +350,32 @@
 
     @pl.when(use_right)
     def _():
+        to_left(last).wait_recv()
+        pairs(
+            mine, 0, stores, clcol_mine, prcol_mine, row_mine,
+            right, last, 1, tag_right, col_right,
+        )
+
+    for e in range(stores):
+        back_mine[e] = finish(row_mine, col_mine, e)
+    for e in range(1, stores):
+        back_copy(0, back_mine, e).start()
+    home[0, s] = back_mine[0]
+
+    @pl.when(use_left)
+    def _():
+        to_right(last).wait_recv()
+        pairs(
+            left, 0, stores, clcol_left, prcol_left, row_left,
+            right, last, 1, tag_right, col_right,
+        )
+        pairs(
+            left, last, 1, clcol_left, prcol_left, row_left,
+            right, 0, last, tag_right, col_right,
+        )
+
+    @pl.when(use_right)
+    def _():
         for e in range(stores):
             back_right[e] = finish(None, col_right, e)
             back_copy(1, back_right, e).start()
@@ -410,12 +455,15 @@
             out_shape=jax.ShapeDtypeStruct((1, rows), f32),
             in_specs=[
                 pl.BlockSpec(memory_space=pl.ANY),
-                pl.BlockSpec(memory_space=vm),
-                pl.BlockSpec(memory_space=vm),
-                pl.BlockSpec(memory_space=vm),
+                pl.BlockSpec(memory_space=pl.ANY),
+                pl.BlockSpec(memory_space=pl.ANY),
+                pl.BlockSpec(memory_space=pl.ANY),
             ],
             out_specs=pl.BlockSpec(memory_space=vm),
             scratch_shapes=[
+                vm((1, rows), i32),
+                vm((1, rows), i32),
+                vm((1, rows), i32),
                 vm((stores, send, width), f32),
                 vm((stores, send, width), bf16),
                 vm((stores, send, width), bf16),
@@ -438,6 +486,7 @@
                 vm((stores, 1, send), f32),
                 vm((3, stores, 1, send), f32),
                 dma((stores,)),
+                dma((3,)),
                 dma((stores,)),
                 dma((stores,)),
                 dma((stores,)),
@@ -452,7 +501,7 @@
                 dma((3, stores)),
             ],
             compiler_params=pltpu.CompilerParams(
-                collective_id=0, has_side_effects=True, vmem_limit_bytes=48 * 1024 * 1024
+                collective_id=0, has_side_effects=True, vmem_limit_bytes=62 * 1024 * 1024
             ),
             name="dedup",
         )(embeddings, slots.reshape(1, rows), clusters, priority)

time: 65.7 us -> 60.8 us (0.925)
  local copies, waits for them, and re-layouts: 4.84 us -> 1.28 us
  Pallas kernels: 60.6 us -> 59.4 us
    unnamed x9 -> x1, local copies, waits for them, and re-layouts: 4.84 us -> 1.28 us
    pallas_call x1, Pallas kernels: 60.6 us -> 59.4 us  [body(): pl.pallas_call(functools.partial(kernel, panels, stores), out_shape=jax.S...]
where the time goes in v2:
time: 60.8 us; the launch traced here: 60.7 us
  Pallas kernels  59.4 us (98%)
  local copies, waits for them, and re-layouts  1.28 us (2%)
    pallas_call x1, Pallas kernels, body(): pl.pallas_call(functools.partial(kernel, panels, stores), out_shape=jax.S...  59.4 us
    unnamed x1, local copies, waits for them, and re-layouts  1.28 us

profile of v2, /device:TPU:0, one launch (start us, length us, event | category | flops | bytes accessed | tf_op | source)
XLA Modules:
  0.0 60.7 jit_solution(6479771978712588609)
XLA Ops:
  0.0 59.4 %dedup.1 = f32[1,1024]{1,0:T(1,128)} custom-call(f32[1024,1024]{1,0:T(8,128)} %emb_ref.1, s32[1,1024]{1,0:T(1,128)} %bitcast.3, s32[1,1024]{1,0:T(1,128)} %cl_hbm.1, s32[1,1024]{1,0:T(1,128)} %pr_hbm.1), custom_call_target="tpu_custom_call" | custom-call | tf_op jit(solution)/shard_map/dedup/pallas_call | solution.py:453
  59.4 1.3 %copy.6 = f32[1024]{0:T(1024)} copy(f32[1024]{0:T(1024)} %bitcast.2) | data formatting | bytes 8192

commit v3 on v2

--- a/solution.py
+++ b/solution.py
@@ -35,9 +35,13 @@
     prcol_mine,
     clcol_left,
     prcol_left,
+    clcol_right,
+    prcol_right,
     row_mine,
     row_left,
+    row_right,
     col_mine,
+    col_left,
     col_right,
     back_mine,
     back_left,
@@ -58,9 +62,11 @@
     bk_send,
     bk_recv,
 ):
-    rows, width = emb.shape[0] * emb.shape[1], emb.shape[2]
+    rows, width = emb.shape
     send = rows // stores
     half = stores // 2
+    last = stores - 1
+    units = send // 128
     p = lax.axis_index("blk")
     s = lax.axis_index("store")
 
@@ -95,13 +101,22 @@
                 barrier, inc=1, device_id={"blk": p + 1, "store": out_peer(d)}, device_id_type=MESH
             )
 
+    pieces = [(k * 128, 128) for k in range(units)]
+    pieces += [(d * send, send) for d in range(1, last)]
+    pieces += [(last * send + k * 128, 128) for k in range(units)]
+
+    def pieces_of(d):
+        return [q for q, (first, _) in enumerate(pieces) if first // send == d]
+
     order = [0, 2, 1] + list(range(3, stores)) if stores > 2 else [0, 1]
 
-    def load(d):
+    def load(d, k=0):
+        count = 128 if d == 0 else send
+        source = pl.multiple_of(out_peer(d) * send, send) + k * 128
         return pltpu.make_async_copy(
-            emb_ref.at[pl.ds(pl.multiple_of(out_peer(d) * send, send), send)],
-            emb.at[d],
-            load_sem.at[d],
+            emb_ref.at[pl.ds(source, count)],
+            emb.at[pl.ds(d * send + k * 128, count)],
+            load_sem.at[k if d == 0 else units - 1 + d],
         )
 
     small = [
@@ -111,7 +126,8 @@
         )
     ]
     for d in order:
-        load(d).start()
+        for k in range(units if d == 0 else 1):
+            load(d, k).start()
     for copy in small:
         copy.start()
 
@@ -119,15 +135,15 @@
     for k in range(3):
         for o in range(stores):
             home[k, o] = low
-    for ref in (row_mine, row_left):
+    for ref in (row_mine, row_left, row_right):
         ref[...] = jnp.full(ref.shape, -1.0, jnp.float32)
-    for ref in (col_mine, col_right):
+    for ref in (col_mine, col_right, col_left):
         ref[...] = jnp.full(ref.shape, -1.0, jnp.float32)
 
     def store_copy(d):
         return pltpu.make_async_remote_copy(
-            src_ref=bound.at[d],
-            dst_ref=mine.at[d],
+            src_ref=bound.at[pl.ds(d * send, send)],
+            dst_ref=mine.at[pl.ds(d * send, send)],
             send_sem=st_send.at[d],
             recv_sem=st_recv.at[d],
             device_id={"store": out_peer(d)},
@@ -144,22 +160,22 @@
             device_id_type=MESH,
         )
 
-    def to_left(d):
-        return pltpu.make_async_remote_copy(
-            src_ref=mine.at[d],
-            dst_ref=right.at[d],
-            send_sem=zl_send.at[d],
-            recv_sem=zl_recv.at[d],
+    def to_left(q):
+        return pltpu.make_async_remote_copy(
+            src_ref=mine.at[pl.ds(*pieces[q])],
+            dst_ref=right.at[pl.ds(*pieces[q])],
+            send_sem=zl_send.at[q],
+            recv_sem=zl_recv.at[q],
             device_id={"blk": p - 1},
             device_id_type=MESH,
         )
 
-    def to_right(d):
-        return pltpu.make_async_remote_copy(
-            src_ref=mine.at[d],
-            dst_ref=left.at[d],
-            send_sem=zr_send.at[d],
-            recv_sem=zr_recv.at[d],
+    def to_right(q):
+        return pltpu.make_async_remote_copy(
+            src_ref=mine.at[pl.ds(*pieces[q])],
+            dst_ref=left.at[pl.ds(*pieces[q])],
+            send_sem=zr_send.at[q],
+            recv_sem=zr_recv.at[q],
             device_id={"blk": p + 1},
             device_id_type=MESH,
         )
@@ -174,36 +190,38 @@
             device_id_type=MESH,
         )
 
-    def forward(d):
+    def forward(these):
         @pl.when(give_right)
         def _():
-            to_right(d).start()
+            for q in these:
+                to_right(q).start()
 
         @pl.when(give_left)
         def _():
-            to_left(d).start()
-
-    def normalize(d):
-        load(d).wait()
-        x = emb[d]
-        unit = (x * lax.rsqrt(jnp.sum(x * x, axis=1, keepdims=True) + EPS)).astype(jnp.bfloat16)
+            for q in these:
+                to_left(q).start()
+
+    def normalize(first, count, into):
+        x = emb[first : first + count, :]
+        unit = x * lax.rsqrt(jnp.sum(x * x, axis=1, keepdims=True) + EPS)
+        into[first : first + count, :] = unit.astype(jnp.bfloat16)
+
+    for d in order:
         if d == 0:
-            mine[0] = unit
-        else:
-            bound[d] = unit
-
-    for number, d in enumerate(order):
-        normalize(d)
-        if number == 0:
-            here = jnp.int32(stores - 1)
-            here = here + jnp.where(has_prev, stores, 0) + jnp.where(has_next, stores, 0)
-            pl.semaphore_wait(barrier, here)
+            for k in range(units):
+                load(0, k).wait()
+                normalize(k * 128, 128, mine)
+                if k == 0:
+                    here = jnp.int32(stores - 1)
+                    here = here + jnp.where(has_prev, stores, 0) + jnp.where(has_next, stores, 0)
+                    pl.semaphore_wait(barrier, here)
+                forward([k])
             small[0].wait()
             for e in range(1, stores):
                 slot_copy(e).start()
-        if d == 0:
-            forward(0)
         else:
+            load(d).wait()
+            normalize(d * send, send, bound)
             store_copy(d).start()
 
     small[1].wait()
@@ -242,32 +260,50 @@
     def _():
         tag_copy(False).start()
 
-    def pairs(a_ref, i, n, clcol, prcol, row_acc, b_ref, j, m, tag_ref, col_acc):
-        a = a_ref[pl.ds(i, n)].reshape(n * send, width)
-        b = b_ref[pl.ds(j, m)].reshape(m * send, width)
+    def score(a, tags_a, row_acc, b, tags_b, col_acc):
         scores = lax.dot_general(
             a, b, (((1,), (1,)), ((), ())), preferred_element_type=jnp.float32
         )
-        for x in range(n):
-            cl_r, pr_r = clcol[i + x], prcol[i + x]
-            best = row_acc[i + x]
-            for y in range(m):
-                for k in range(send // 128):
-                    part = slice(k * 128, (k + 1) * 128)
-                    cl_q = tag_ref[j + y, 0:1, part]
-                    pr_q = tag_ref[j + y, 1:2, part]
-                    piece = scores[
-                        x * send : (x + 1) * send, y * send + k * 128 : y * send + (k + 1) * 128
-                    ]
-                    same = jnp.where(cl_r == cl_q, piece, -1.0)
-                    best = jnp.maximum(best, jnp.where(pr_q < pr_r, same, -1.0))
-                    other = jnp.where(pr_q > pr_r, same, -1.0)
-                    top = jnp.max(other.reshape(send // 8, 8, 128), axis=0)
-                    col_acc[j + y, :, part] = jnp.maximum(col_acc[j + y, :, part], top)
-            row_acc[i + x] = best
+        cl_r, pr_r = tags_a
+        best = row_acc[...]
+        for c in range(b.shape[0] // 128):
+            cl_q, pr_q = tags_b(c)
+            same = jnp.where(cl_r == cl_q, scores[:, c * 128 : (c + 1) * 128], -1.0)
+            best = jnp.maximum(best, jnp.where(pr_q < pr_r, same, -1.0))
+            other = jnp.where(pr_q > pr_r, same, -1.0)
+            col_acc(c, jnp.max(other.reshape(a.shape[0] // 8, 8, 128), axis=0))
+        row_acc[...] = best
+
+    def chunk(ref, i):
+        return ref[pl.ds(pl.multiple_of(i * send, send), send), :]
+
+    def tags_from(tag_ref, j):
+        def at(c):
+            part = slice(c % units * 128, c % units * 128 + 128)
+            return tag_ref[j + c // units, 0:1, part], tag_ref[j + c // units, 1:2, part]
+
+        return at
+
+    def best_into(acc, j):
+        def at(c, top):
+            part = slice(c % units * 128, c % units * 128 + 128)
+            acc[j + c // units, :, part] = jnp.maximum(acc[j + c // units, :, part], top)
+
+        return at
 
     def pair(a_ref, i, clcol, prcol, row_acc, b_ref, j, tag_ref, col_acc):
-        pairs(a_ref, i, 1, clcol, prcol, row_acc, b_ref, j, 1, tag_ref, col_acc)
+        score(
+            chunk(a_ref, i), (clcol[i], prcol[i]), row_acc.at[i],
+            chunk(b_ref, j), tags_from(tag_ref, j), best_into(col_acc, j),
+        )
+
+    def strip(a_ref, k, clcol, prcol, row_acc, b_ref, count, tag_ref, col_acc):
+        part = pl.ds(k * 128, 128)
+        score(
+            a_ref[last * send + k * 128 : last * send + k * 128 + 128, :],
+            (clcol[last, part], prcol[last, part]), row_acc.at[last, part],
+            b_ref[0:count, :], tags_from(tag_ref, 0), best_into(col_acc, 0),
+        )
 
     def loop(count, step):
         def each(i, carry):
@@ -279,7 +315,7 @@
     for d in range(stores):
         if d > 0:
             store_copy(d).wait_recv()
-            forward(d)
+            forward(pieces_of(d))
         loop(
             d + 1,
             lambda i, d=d: pair(
@@ -287,14 +323,6 @@
             ),
         )
 
-    def finish(acc_row, acc_col, d):
-        parts = []
-        if acc_row is not None:
-            parts.append(jnp.max(jnp.transpose(acc_row[d]), axis=0, keepdims=True))
-        if acc_col is not None:
-            parts.append(jnp.max(acc_col[d], axis=0, keepdims=True))
-        return functools.reduce(jnp.maximum, parts)
-
     def back_copy(kind, src, d):
         where = {"store": in_peer(d)}
         if kind:
@@ -317,13 +345,14 @@
     @pl.when(use_right)
     def _():
         tag_copy(False).wait_recv()
-
-    last = stores - 1
+        columns(tag_right, clcol_right, prcol_right, last)
+
     for d in range(last):
 
         @pl.when(use_right)
         def _(d=d):
-            to_left(d).wait_recv()
+            for q in pieces_of(d):
+                to_left(q).wait_recv()
             loop(
                 stores,
                 lambda i: pair(
@@ -333,7 +362,8 @@
 
         @pl.when(use_left)
         def _(d=d):
-            to_right(d).wait_recv()
+            for q in pieces_of(d):
+                to_right(q).wait_recv()
             loop(
                 d + 1,
                 lambda i: pair(
@@ -348,42 +378,58 @@
                     ),
                 )
 
+    def turned(acc, d):
+        return jnp.max(jnp.transpose(acc[d]), axis=0, keepdims=True)
+
+    def over_rows(acc, d):
+        return jnp.max(acc[d], axis=0, keepdims=True)
+
+    for k, q in enumerate(pieces_of(last)):
+        if k == units - 1:
+            for e in range(stores):
+                back_mine[e] = turned(row_mine, e)
+            for e in range(last):
+                back_left[e] = turned(row_left, e)
+
+        @pl.when(use_right)
+        def _(k=k, q=q):
+            to_left(q).wait_recv()
+            strip(
+                right, k, clcol_right, prcol_right, row_right, mine, rows, tag_mine, col_mine
+            )
+
+        @pl.when(use_left)
+        def _(k=k, q=q):
+            to_right(q).wait_recv()
+            strip(
+                right, k, clcol_right, prcol_right, row_right,
+                left, last * send + k * 128 + 128, tag_left, col_left,
+            )
+            strip(
+                left, k, clcol_left, prcol_left, row_left,
+                right, last * send + k * 128, tag_right, col_right,
+            )
+
+    for e in range(stores):
+        back_mine[e] = jnp.maximum(back_mine[e], over_rows(col_mine, e))
+        if e > 0:
+            back_copy(0, back_mine, e).start()
+    home[0, s] = back_mine[0]
+
     @pl.when(use_right)
     def _():
-        to_left(last).wait_recv()
-        pairs(
-            mine, 0, stores, clcol_mine, prcol_mine, row_mine,
-            right, last, 1, tag_right, col_right,
-        )
-
-    for e in range(stores):
-        back_mine[e] = finish(row_mine, col_mine, e)
-    for e in range(1, stores):
-        back_copy(0, back_mine, e).start()
-    home[0, s] = back_mine[0]
+        for e in range(stores):
+            best = over_rows(col_right, e)
+            if e == last:
+                best = jnp.maximum(best, turned(row_right, e))
+            back_right[e] = best
+            back_copy(1, back_right, e).start()
 
     @pl.when(use_left)
     def _():
-        to_right(last).wait_recv()
-        pairs(
-            left, 0, stores, clcol_left, prcol_left, row_left,
-            right, last, 1, tag_right, col_right,
-        )
-        pairs(
-            left, last, 1, clcol_left, prcol_left, row_left,
-            right, 0, last, tag_right, col_right,
-        )
-
-    @pl.when(use_right)
-    def _():
         for e in range(stores):
-            back_right[e] = finish(None, col_right, e)
-            back_copy(1, back_right, e).start()
-
-    @pl.when(use_left)
-    def _():
-        for e in range(stores):
-            back_left[e] = finish(row_left, None, e)
+            before = turned(row_left, e) if e == last else back_left[e]
+            back_left[e] = jnp.maximum(before, over_rows(col_left, e))
             back_copy(2, back_left, e).start()
 
     for d in range(1, stores):
@@ -392,14 +438,14 @@
     @pl.when(give_right)
     def _():
         tag_copy(True).wait_send()
-        for d in range(stores):
-            to_right(d).wait_send()
+        for q in range(len(pieces)):
+            to_right(q).wait_send()
 
     @pl.when(give_left)
     def _():
         tag_copy(False).wait_send()
-        for d in range(stores):
-            to_left(d).wait_send()
+        for q in range(len(pieces)):
+            to_left(q).wait_send()
 
     def arrived(kind, o):
         return pltpu.make_async_remote_copy(
@@ -447,6 +493,7 @@
     def body(embeddings, slots, clusters, priority):
         rows, width = embeddings.shape
         send = rows // stores
+        units = send // 128
         f32, bf16, i32 = jnp.float32, jnp.bfloat16, jnp.int32
         vm = pltpu.VMEM
         dma = pltpu.SemaphoreType.DMA
@@ -464,11 +511,11 @@
                 vm((1, rows), i32),
                 vm((1, rows), i32),
                 vm((1, rows), i32),
-                vm((stores, send, width), f32),
-                vm((stores, send, width), bf16),
-                vm((stores, send, width), bf16),
-                vm((stores, send, width), bf16),
-                vm((stores, send, width), bf16),
+                vm((rows, width), f32),
+                vm((rows, width), bf16),
+                vm((rows, width), bf16),
+                vm((rows, width), bf16),
+                vm((rows, width), bf16),
                 vm((stores, 1, send), i32),
                 vm((stores, 8, send), f32),
                 vm((stores, 8, send), f32),
@@ -479,13 +526,17 @@
                 vm((stores, send, 128), f32),
                 vm((stores, send, 128), f32),
                 vm((stores, send, 128), f32),
+                vm((stores, send, 128), f32),
+                vm((stores, send, 128), f32),
+                vm((stores, send, 128), f32),
+                vm((stores, 8, send), f32),
                 vm((stores, 8, send), f32),
                 vm((stores, 8, send), f32),
                 vm((stores, 1, send), f32),
                 vm((stores, 1, send), f32),
                 vm((stores, 1, send), f32),
                 vm((3, stores, 1, send), f32),
-                dma((stores,)),
+                dma((stores + units - 1,)),
                 dma((3,)),
                 dma((stores,)),
                 dma((stores,)),
@@ -493,10 +544,10 @@
                 dma((stores,)),
                 dma((2,)),
                 dma((2,)),
-                dma((stores,)),
-                dma((stores,)),
-                dma((stores,)),
-                dma((stores,)),
+                dma((stores - 2 + 2 * units,)),
+                dma((stores - 2 + 2 * units,)),
+                dma((stores - 2 + 2 * units,)),
+                dma((stores - 2 + 2 * units,)),
                 dma((3, stores)),
                 dma((3, stores)),
             ],

time: 60.8 us -> 60.7 us (level)
  no operation moved by 1% of the time
where the time goes in v3:
time: 60.7 us; the launch traced here: 60.5 us
  Pallas kernels  59.2 us (98%)
  local copies, waits for them, and re-layouts  1.28 us (2%)
    pallas_call x1, Pallas kernels, body(): pl.pallas_call(functools.partial(kernel, panels, stores), out_shape=jax.S...  59.2 us
    unnamed x1, local copies, waits for them, and re-layouts  1.28 us

profile of v3, /device:TPU:0, one launch (start us, length us, event | category | flops | bytes accessed | tf_op | source)
XLA Modules:
  0.0 60.5 jit_solution(2220499710138801796)
XLA Ops:
  0.0 59.2 %dedup.1 = f32[1,1024]{1,0:T(1,128)} custom-call(f32[1024,1024]{1,0:T(8,128)} %emb_ref.1, s32[1,1024]{1,0:T(1,128)} %bitcast.3, s32[1,1024]{1,0:T(1,128)} %cl_hbm.1, s32[1,1024]{1,0:T(1,128)} %pr_hbm.1), custom_call_target="tpu_custom_call" | custom-call | tf_op jit(solution)/shard_map/dedup/pallas_call | solution.py:500
  59.2 1.3 %copy.6 = f32[1024]{0:T(1024)} copy(f32[1024]{0:T(1024)} %bitcast.2) | data formatting | bytes 8192

commit v4 on v3

--- a/solution.py
+++ b/solution.py
@@ -79,8 +79,9 @@
     has_prev = p >= 1
     has_next = p <= panels - 2
     use_right = has_next
-    use_left = jnp.logical_and(has_prev, has_next)
-    give_right = p <= panels - 3
+    use_left = has_prev
+    use_both = jnp.logical_and(has_prev, has_next)
+    give_right = has_next
     give_left = has_prev
 
     barrier = pltpu.get_barrier_semaphore()
@@ -190,14 +191,22 @@
             device_id_type=MESH,
         )
 
-    def forward(these):
+    waited = set()
+
+    def forward(these, after=()):
+        waited.update(after)
+
         @pl.when(give_right)
         def _():
+            for q in after:
+                to_right(q).wait_send()
             for q in these:
                 to_right(q).start()
 
         @pl.when(give_left)
         def _():
+            for q in after:
+                to_left(q).wait_send()
             for q in these:
                 to_left(q).start()
 
@@ -222,7 +231,8 @@
         else:
             load(d).wait()
             normalize(d * send, send, bound)
-            store_copy(d).start()
+            if d <= 2:
+                store_copy(d).start()
 
     small[1].wait()
     small[2].wait()
@@ -297,12 +307,12 @@
             chunk(b_ref, j), tags_from(tag_ref, j), best_into(col_acc, j),
         )
 
-    def strip(a_ref, k, clcol, prcol, row_acc, b_ref, count, tag_ref, col_acc):
+    def strip(a_ref, k, clcol, prcol, row_acc, b_ref, j, first, count, tag_ref, col_acc):
         part = pl.ds(k * 128, 128)
         score(
             a_ref[last * send + k * 128 : last * send + k * 128 + 128, :],
             (clcol[last, part], prcol[last, part]), row_acc.at[last, part],
-            b_ref[0:count, :], tags_from(tag_ref, 0), best_into(col_acc, 0),
+            b_ref[first : first + count, :], tags_from(tag_ref, j), best_into(col_acc, j),
         )
 
     def loop(count, step):
@@ -314,8 +324,12 @@
 
     for d in range(stores):
         if d > 0:
+            if 2 <= d < last:
+                store_copy(d).wait_send()
+                store_copy(d + 1).start()
             store_copy(d).wait_recv()
-            forward(pieces_of(d))
+            if d < last:
+                forward(pieces_of(d))
         loop(
             d + 1,
             lambda i, d=d: pair(
@@ -348,6 +362,10 @@
         columns(tag_right, clcol_right, prcol_right, last)
 
     for d in range(last):
+        if d == last - 2:
+            forward(pieces_of(last)[:1], pieces_of(d))
+        if d == last - 1:
+            forward(pieces_of(last)[1:], pieces_of(d))
 
         @pl.when(use_right)
         def _(d=d):
@@ -364,6 +382,10 @@
         def _(d=d):
             for q in pieces_of(d):
                 to_right(q).wait_recv()
+            pair(left, d, clcol_left, prcol_left, row_left, mine, last, tag_mine, col_mine)
+
+        @pl.when(use_both)
+        def _(d=d):
             loop(
                 d + 1,
                 lambda i: pair(
@@ -392,22 +414,26 @@
                 back_left[e] = turned(row_left, e)
 
         @pl.when(use_right)
-        def _(k=k, q=q):
+        def _(q=q):
             to_left(q).wait_recv()
-            strip(
-                right, k, clcol_right, prcol_right, row_right, mine, rows, tag_mine, col_mine
-            )
 
         @pl.when(use_left)
         def _(k=k, q=q):
             to_right(q).wait_recv()
             strip(
+                left, k, clcol_left, prcol_left, row_left,
+                mine, last, last * send, send, tag_mine, col_mine,
+            )
+
+        @pl.when(use_both)
+        def _(k=k):
+            strip(
                 right, k, clcol_right, prcol_right, row_right,
-                left, last * send + k * 128 + 128, tag_left, col_left,
+                left, 0, 0, last * send + k * 128 + 128, tag_left, col_left,
             )
             strip(
                 left, k, clcol_left, prcol_left, row_left,
-                right, last * send + k * 128, tag_right, col_right,
+                right, 0, 0, last * send + k * 128, tag_right, col_right,
             )
 
     for e in range(stores):
@@ -433,19 +459,22 @@
             back_copy(2, back_left, e).start()
 
     for d in range(1, stores):
-        store_copy(d).wait_send()
+        if d < 2 or d == last:
+            store_copy(d).wait_send()
 
     @pl.when(give_right)
     def _():
         tag_copy(True).wait_send()
         for q in range(len(pieces)):
-            to_right(q).wait_send()
+            if q not in waited:
+                to_right(q).wait_send()
 
     @pl.when(give_left)
     def _():
         tag_copy(False).wait_send()
         for q in range(len(pieces)):
-            to_left(q).wait_send()
+            if q not in waited:
+                to_left(q).wait_send()
 
     def arrived(kind, o):
         return pltpu.make_async_remote_copy(

time: 60.7 us -> 60 us (0.988)
    pallas_call x1, Pallas kernels: 59.2 us -> 58.6 us  [body(): pl.pallas_call(functools.partial(kernel, panels, stores), out_shape=jax.S...]
where the time goes in v4:
time: 60 us; the launch traced here: 59.9 us
  Pallas kernels  58.6 us (98%)
  local copies, waits for them, and re-layouts  1.28 us (2%)
    pallas_call x1, Pallas kernels, body(): pl.pallas_call(functools.partial(kernel, panels, stores), out_shape=jax.S...  58.6 us
    unnamed x1, local copies, waits for them, and re-layouts  1.28 us

profile of v4, /device:TPU:0, one launch (start us, length us, event | category | flops | bytes accessed | tf_op | source)
XLA Modules:
  0.0 59.9 jit_solution(8829201680492702502)
XLA Ops:
  0.0 58.6 %dedup.1 = f32[1,1024]{1,0:T(1,128)} custom-call(f32[1024,1024]{1,0:T(8,128)} %emb_ref.1, s32[1,1024]{1,0:T(1,128)} %bitcast.3, s32[1,1024]{1,0:T(1,128)} %cl_hbm.1, s32[1,1024]{1,0:T(1,128)} %pr_hbm.1), custom_call_target="tpu_custom_call" | custom-call | tf_op jit(solution)/shard_map/dedup/pallas_call | solution.py:529
  58.6 1.3 %copy.6 = f32[1024]{0:T(1024)} copy(f32[1024]{0:T(1024)} %bitcast.2) | data formatting | bytes 8192
